TPU v7x, 256 devices: a whole 4x4x8 slice. The times are simulated.
256 devices in a mesh: layer: 64 (over x, z, core), col: 4 (over y).
Axes of the slice: x: 4, y: 4, z: 8, core: 2. Of those that a mesh axis runs over, the one named last changes fastest.
Arguments:
- l_panels: bfloat16 [64, 2048, 2048], P('layer', None, 'col'), may hold values from -6 to 6
- u_panels: bfloat16 [64, 2048, 2048], P('layer', None, 'col'), may hold values from -0.125 to 0.125
- l_masks: int32 [64, 8, 8], P('layer'), may hold values 0 or 1
- u_masks: int32 [64, 8, 8], P('layer'), may hold values 0 or 1
- ancestor_tiles: int32 [8, 8], replicated, may hold values 0 or 1
- initial: float32 [2048, 2048], P('layer', 'col'), may hold values from -6 to 6
Outputs:
- schur: float32 [2048, 2048], P('layer', 'col')
All inputs are finite; a program needn't handle non-finite values. No bound on the sum of `l_masks` or of `u_masks` on one device may be relied on, other than what follows from the above.
Results may differ from a plain program's by a relative error of at most 0.0003.
Values may be sent and summed in bfloat16 or wider, within the bound.
A program may use at most 64 MiB of HBM per device.

v0:
```python
import jax
import jax.numpy as jnp
from jax import lax
from jax.sharding import PartitionSpec as P

TILE = 256


def expand_tiles(mask):
    return jnp.repeat(jnp.repeat(mask, TILE, 0), TILE, 1)


def local(l_panels, u_panels, l_masks, u_masks, ancestor_tiles, initial):
    col_index = lax.axis_index("col")
    depth_cols = l_panels.shape[2]
    width_cols = u_panels.shape[2]
    row_count = initial.shape[0]
    lmask_mine = lax.dynamic_slice_in_dim(
        l_masks[0], col_index * (depth_cols // TILE), depth_cols // TILE, 1
    )
    lpanel = l_panels[0] * expand_tiles(lmask_mine).astype(jnp.bfloat16)
    umask_mine = lax.dynamic_slice_in_dim(
        u_masks[0], col_index * (width_cols // TILE), width_cols // TILE, 1
    )
    upanel = u_panels[0] * expand_tiles(umask_mine).astype(jnp.bfloat16)
    full_panel = lax.all_gather(lpanel, "col", axis=1, tiled=True)
    product = jnp.dot(full_panel, upanel, preferred_element_type=jnp.float32)
    summed = lax.psum_scatter(product, "layer", scatter_dimension=0, tiled=True)
    row_ids = lax.axis_index("layer") * row_count + jnp.arange(row_count, dtype=jnp.int32)
    tile_ids = jnp.arange(ancestor_tiles.shape[0], dtype=jnp.int32)
    onehot = (row_ids[:, None] // TILE == tile_ids[None, :]).astype(jnp.float32)
    row_pattern = jnp.dot(
        onehot, ancestor_tiles.astype(jnp.float32), preferred_element_type=jnp.float32
    )
    col_pattern = lax.dynamic_slice_in_dim(
        row_pattern, col_index * (width_cols // TILE), width_cols // TILE, 1
    )
    pattern = jnp.repeat(col_pattern, TILE, 1)
    return initial - pattern * summed


def solution(mesh):
    return jax.shard_map(
        local,
        mesh=mesh,
        in_specs=(
            P("layer", None, "col"),
            P("layer", None, "col"),
            P("layer", None, None),
            P("layer", None, None),
            P(),
            P("layer", "col"),
        ),
        out_specs=P("layer", "col"),
        check_vma=False,
    )
```

profile of v0, /device:TPU:1, one launch (start us, length us, event | category | flops | bytes accessed | tf_op | source)
XLA Modules:
  0.0 261.4 jit_solution(10379563578866441089)
XLA Ops:
  6.5 0.0 all-gather.2.cloned.1.call-start
  6.5 0.8 fusion.4
  7.3 0.1 broadcast_in_dim.18
  7.4 2.5 broadcast_in_dim.19
  9.9 0.0 copy-start
  9.9 0.5 copy.15
  10.4 1.1 copy-done
  11.5 1.6 bitcast_multiply_fusion.2
  13.0 0.0 all-gather.2.cloned.1.call-update
  13.1 0.0 reduce-scatter.2.cloned.1.call-start
  13.1 0.1 broadcast_in_dim.20
  13.2 2.5 broadcast_in_dim.21
  15.7 0.5 copy.16
  16.2 86.5 %all-gather.2.cloned.1.call-done = bf16[2048,2048]{1,0:T(8,128)(2,1)} async-done(((bf16[2048,512]{1,0:T(8,128)(2,1)}), bf16[2048,2048]{1,0:T(8,128)(2,1)}) %all-gather.2.cloned.1.call-update) | async-done | bytes 8388624 | tf_op jit(solution)/shard_map/all_gather | solution.py:26
  102.7 10.5 %fusion = f32[2048,512]{1,0:T(8,128)} fusion(bf16[2048,2048]{1,0:T(8,128)(2,1)} %all-gather.2.cloned.1.call-done, bf16[2048,512]{1,0:T(8,128)(2,1)S(1)} %bitcast.23, bf16[1,2048,512]{2,1,0:T(8,128)(2,1)} %param.7), kind=kOutput, calls=%fused_computation.1 | convolution fusion | flops 4296015872 | bytes 16777216 | tf_op jit(solution)/shard_map/dot_general | solution.py:27
  113.1 0.0 copy-start.2
  113.2 0.0 reduce-scatter.2.cloned.1.call-update
  113.2 0.6 copy-done.2
  113.8 0.2 fusion.1
  114.0 0.1 copy.7
  114.1 0.1 broadcast_in_dim.17
  114.3 138.8 %reduce-scatter.2.cloned.1.call-done = f32[32,512]{1,0:T(8,128)} async-done(((f32[2048,512]{1,0:T(8,128)}), f32[32,512]{1,0:T(8,128)}) %reduce-scatter.2.cloned.1.call-update) | async-done | bytes 65552 | tf_op jit(solution)/shard_map/reduce_scatter | solution.py:28
  253.0 0.0 copy-done.1
  253.0 1.5 multiply_subtract_fusion
  (4 shorter events, 0.0 us)
Async XLA Ops:
  6.5 96.1 %all-gather.2.cloned.1.call-start = ((), (), s32[]{:S(2)}) async-start(), calls=%async_computation.1 | async-start | bytes 10485760 | tf_op jit(solution)/shard_map/all_gather | solution.py:26
  9.9 1.6 copy-start
  13.1 240.0 %reduce-scatter.2.cloned.1.call-start = ((), (), s32[]{:S(2)}) async-start(), calls=%async_computation.2 | async-start | bytes 4259840 | tf_op jit(solution)/shard_map/reduce_scatter | solution.py:28
  113.1 0.7 copy-start.2
  113.2 139.9 %copy-start.1 = (f32[32,512]{1,0:T(8,128)S(1)}, f32[32,512]{1,0:T(8,128)}, u32[]{:S(2)}) copy-start(f32[32,512]{1,0:T(8,128)} %param.11) | copy-start | bytes 196612
Sparse Core Ops, SparseCore 0:
  13.2 89.4 all-gather.1
  113.3 139.6 reduce-scatter.1
where the time goes:
time: 266 us; the launch traced here: 261 us
  waiting for transfers between devices  225 us (85%)
  between operations  13.5 us (5%)
  matrix products  10.6 us (4%)
  local copies, waits for them, and re-layouts  8.05 us (3%)
  other arithmetic  3.83 us (1%)
    reduce_scatter x1, waiting for transfers between devices, local(): summed = lax.psum_scatter(product, 'layer', scatter_dimension=0, tiled=True)  139 us
    all_gather x1, waiting for transfers between devices, local(): full_panel = lax.all_gather(lpanel, 'col', axis=1, tiled=True)  86.5 us
    dot_general x1, matrix products, local(): product = jnp.dot(full_panel, upanel, preferred_element_type=jnp.float32)  10.5 us
  transfers between devices with their start and end apart: 2, of which 2 were waited for; matrix products, arithmetic and copies ran while one was open for 1% of the time, Pallas kernels for 0%

commit v1 on v0

v1 whole, which is shorter than its diff:
```python
import jax
import jax.numpy as jnp
from jax import lax
from jax.experimental import pallas as pl
from jax.experimental.pallas import tpu as pltpu
from jax.sharding import PartitionSpec as P

MESH = pl.DeviceIdType.MESH
TILE = 256
NX, NY, NZ = 4, 4, 8
DEPTH = 512
PIECE = 256
CHUNK = 64
CODES = 16
LEVELS = 32000.0
STEPS = 8.0


def encode(block, codes, where):
    rows, cols = block.shape
    top = jnp.maximum(jnp.max(jnp.abs(block), axis=0, keepdims=True), 2.0**-100)
    level = jnp.ceil(jnp.log2(top) * STEPS) + 1.0
    factor = jnp.exp2(level * (-1.0 / STEPS)) * LEVELS
    codes[(*where, pl.ds(0, rows), slice(None))] = jnp.round(block * factor).astype(jnp.int32).astype(jnp.int16)
    codes[(*where, pl.ds(rows, CODES), slice(None))] = (
        jnp.broadcast_to(level, (CODES, cols)).astype(jnp.int32).astype(jnp.int16)
    )


def decode(codes, where, rows):
    level = codes[(*where, pl.ds(rows, CODES), slice(None))].astype(jnp.int32).astype(jnp.float32)[0:1]
    factor = jnp.exp2(level * (1.0 / STEPS)) * (1.0 / LEVELS)
    return codes[(*where, pl.ds(0, rows), slice(None))].astype(jnp.int32).astype(jnp.float32) * factor


def kernel(
    l_hbm, u_hbm, lmask, umask, ancestor, initial, out,
    lbuf, uown, ubuf, part, x1s, x1r, x2s, x2r, ssum, zs, zr, ys, yr, total, cs, cr,
    in_sem, a_send, a_recv, l_send, l_recv, x1_send, x1_recv, x2_send, x2_recv,
    z_send, z_recv, y_send, y_recv, c_send, c_recv,
):
    layer = lax.axis_index("layer")
    y = lax.axis_index("col")
    x = layer // (2 * NZ)
    z = (layer // 2) % NZ
    core = layer % 2
    xa = x + 1 - 2 * (x % 2)
    xb = 3 - x
    xd = 3 - xa

    def at(x_, y_, z_, c_):
        return ((x_ * NZ + z_) * 2 + c_, y_)

    def ydev(step, k):
        return at(x, (y + step) % NY, z, (core + k) % 2)

    sibling = at(x, y, z, 1 - core)
    partners = [sibling]
    partners += [ydev(step, k) for step in (1, 2, 3) for k in (0, 1)]
    partners += [at(xa, y, z, core), at(xb, y, z, core)]
    partners += [at(x, y, (z + i) % NZ, core) for i in range(1, NZ)]
    partners += [at(x, (y + 2) % NY, (z + i) % NZ, core) for i in range(1, NZ)]

    def rows_of(first, count):
        return pl.ds(pl.multiple_of(first, count), count)

    u_order = [(y + step) % NY for step in (1, 3, 2, 0)]
    l_order = [xd, xa, xb, x]
    u_in = [
        pltpu.make_async_copy(u_hbm.at[0, rows_of(b * DEPTH, DEPTH)], uown.at[rows_of(b * DEPTH, DEPTH)], in_sem.at[n])
        for n, b in enumerate(u_order)
    ]
    l_in = [
        pltpu.make_async_copy(l_hbm.at[0, rows_of(b * DEPTH, DEPTH)], lbuf.at[0, rows_of(b * DEPTH, DEPTH)], in_sem.at[4 + n])
        for n, b in enumerate(l_order)
    ]
    for n in range(4):
        u_in[n].start()
        l_in[n].start()
    barrier = pltpu.get_barrier_semaphore()
    for partner in partners:
        pl.semaphore_signal(barrier, inc=1, device_id=partner, device_id_type=MESH)

    def mask_u(block):
        for t in range(2):
            rows = rows_of(block * DEPTH + t * TILE, TILE)
            for h in range(2):
                keep = umask[0, block * 2 + t, y * 2 + h].astype(jnp.float32)
                cols = pl.ds(h * TILE, TILE)
                uown[rows, cols] = uown[rows, cols] * jnp.full((TILE, TILE), keep).astype(jnp.bfloat16)

    def mask_l(block):
        for t in range(2):
            rows = rows_of(block * DEPTH + t * TILE, TILE)
            for h in range(2):
                keep = lmask[0, block * 2 + t, y * 2 + h].astype(jnp.float32)
                cols = pl.ds(h * TILE, TILE)
                lbuf[0, rows, cols] = lbuf[0, rows, cols] * jnp.full((TILE, TILE), keep).astype(jnp.bfloat16)

    def send_u(step, k):
        block = (y + step) % NY
        to = (core + k) % 2
        slot = (NY - step) % NY
        src = uown.at[rows_of(block * DEPTH, DEPTH), pl.ds(pl.multiple_of(to * TILE, TILE), TILE)]
        return pltpu.make_async_remote_copy(
            src, ubuf.at[slot, k], a_send.at[slot * 2 + k], a_recv.at[slot * 2 + k],
            device_id=ydev(step, k), device_id_type=MESH,
        )

    def send_l(n):
        rows = rows_of(l_order[n] * DEPTH, DEPTH)
        return pltpu.make_async_remote_copy(
            lbuf.at[0, rows], lbuf.at[1, rows], l_send.at[n], l_recv.at[n], device_id=sibling, device_id_type=MESH,
        )

    u_in[0].wait()
    mask_u(u_order[0])
    u_in[1].wait()
    mask_u(u_order[1])
    pl.semaphore_wait(barrier, len(partners))
    for step in (1, 3):
        for k in range(2):
            send_u(step, k).start()
    u_in[3].wait()
    mask_u(u_order[3])
    send_u(0, 1).start()
    for n in range(4):
        l_in[n].wait()
        mask_l(l_order[n])
        send_l(n).start()
    u_in[2].wait()
    mask_u(u_order[2])
    for k in range(2):
        send_u(2, k).start()
    own = uown[rows_of(y * DEPTH, DEPTH), pl.ds(pl.multiple_of(core * TILE, TILE), TILE)]
    ubuf[0, 0] = own

    def product(s, first):
        rows = rows_of(first, PIECE)
        return jnp.dot(lbuf[0, rows], ubuf[s, 0], preferred_element_type=jnp.float32) + jnp.dot(
            lbuf[1, rows], ubuf[s, 1], preferred_element_type=jnp.float32
        )

    def x1_copy(s, q):
        return pltpu.make_async_remote_copy(
            x1s.at[s, q], x1r.at[s, q], x1_send.at[s * 2 + q], x1_recv.at[s * 2 + q],
            device_id=at(xb if q else xa, y, z, core), device_id_type=MESH,
        )

    def x2_copy(s, q):
        return pltpu.make_async_remote_copy(
            x2s.at[s, q], x2r.at[s, q], x2_send.at[s * 2 + q], x2_recv.at[s * 2 + q],
            device_id=at(xa if q else xb, y, z, core), device_id_type=MESH,
        )

    def z_copy(s, i):
        return pltpu.make_async_remote_copy(
            zs.at[s, i], zr.at[s, i], z_send.at[s * NZ + i], z_recv.at[s * NZ + i],
            device_id=at(x, (y + 2) % NY if s == 2 else y, (z + i) % NZ, core), device_id_type=MESH,
        )

    def y_copy(n):
        return pltpu.make_async_remote_copy(
            ys.at[n], yr.at[n], y_send.at[n], y_recv.at[n], device_id=ydev((1, 3)[n], 0), device_id_type=MESH,
        )

    def multiply(s):
        for q in range(2):
            for i in range(2):
                goal = xd if i else (xb if q else xa)
                encode(product(s, goal * 2 * PIECE + q * PIECE), x1s, (s, q, i))
            x1_copy(s, q).start()
        for q in range(2):
            for i in range(2):
                goal = ((xa if q else xb) if i else x)
                part[s, q, i] = product(s, goal * 2 * PIECE + q * PIECE)

    def after_x1(s):
        for q in range(2):
            x1_copy(s, q).wait_recv()
            encode(part[s, q, 1] + decode(x1r, (s, q, 1), PIECE), x2s, (s, q))
            x2_copy(s, q).start()
        for q in range(2):
            part[s, q, 0] = part[s, q, 0] + decode(x1r, (s, q, 0), PIECE)

    hops = {2: (4, 3, 5, 2, 6, 1, 7, 0)}

    def after_x2(s):
        for q in range(2):
            x2_copy(s, q).wait_recv()
            ssum[s, pl.ds(q * PIECE, PIECE)] = part[s, q, 0] + decode(x2r, (s, q), PIECE)
        for i in hops.get(s, (4, 3, 5, 2, 6, 1, 7)):
            encode(ssum[s, rows_of((z + i) % NZ * CHUNK, CHUNK)], zs, (s, i))
            z_copy(s, i).start()

    def after_z(s):
        result = None if s == 2 else ssum[s, rows_of(z * CHUNK, CHUNK)]
        for i in (1, 7, 2, 6, 3, 5, 4, 0) if s == 2 else (1, 7, 2, 6, 3, 5, 4):
            z_copy(s, i).wait_recv()
            piece = decode(zr, (s, i), CHUNK)
            result = piece if result is None else result + piece
        return result

    def arrived(s):
        for k in range(2):
            send_u((NY - s) % NY, k).wait_recv()

    send_u(0, 1).wait_recv()
    for n in range(4):
        send_l(n).wait_recv()
    multiply(0)
    after_x1(0)
    arrived(1)
    multiply(1)
    arrived(3)
    multiply(3)
    after_x2(0)
    after_x1(1)
    after_x1(3)
    arrived(2)
    multiply(2)
    total[...] = after_z(0)
    after_x2(1)
    after_x2(3)
    after_x1(2)
    ys[0] = after_z(1)
    y_copy(0).start()
    ys[1] = after_z(3)
    y_copy(1).start()
    after_x2(2)
    for n in range(2):
        y_copy(n).wait_recv()
    total[...] = total[...] + yr[0] + yr[1] + after_z(2)
    half = CHUNK // 2
    cs[...] = total[rows_of((1 - core) * half, half)]
    across = pltpu.make_async_remote_copy(cs, cr, c_send.at[0], c_recv.at[0], device_id=sibling, device_id_type=MESH)
    across.start()

    def finish(side, value):
        keep = ancestor[layer // (TILE // half), y * 2 + side].astype(jnp.float32)
        cols = pl.ds(pl.multiple_of(side * TILE, TILE), TILE)
        out[:, cols] = initial[:, cols] - keep * value

    finish(core, total[rows_of(core * half, half)])
    across.wait_recv()
    finish(1 - core, cr[...])

    for step in (1, 3, 2):
        for k in range(2):
            send_u(step, k).wait_send()
    send_u(0, 1).wait_send()
    for n in range(4):
        send_l(n).wait_send()
    for s in range(4):
        for q in range(2):
            x1_copy(s, q).wait_send()
            x2_copy(s, q).wait_send()
        for i in range(0 if s == 2 else 1, NZ):
            z_copy(s, i).wait_send()
    for n in range(2):
        y_copy(n).wait_send()
    across.wait_send()


def local(l_panels, u_panels, l_masks, u_masks, ancestor_tiles, initial):
    any_spec = pl.BlockSpec(memory_space=pl.ANY)
    smem = pl.BlockSpec(memory_space=pltpu.SMEM)
    vmem = pl.BlockSpec(memory_space=pltpu.VMEM)
    dma = pltpu.SemaphoreType.DMA
    bf16, f32, i16 = jnp.bfloat16, jnp.float32, jnp.int16
    return pl.pallas_call(
        kernel,
        out_shape=jax.ShapeDtypeStruct(initial.shape, f32),
        in_specs=[any_spec, any_spec, smem, smem, smem, vmem],
        out_specs=vmem,
        scratch_shapes=[
            pltpu.VMEM((2, 2048, DEPTH), bf16),
            pltpu.VMEM((2048, DEPTH), bf16),
            pltpu.VMEM((NY, 2, DEPTH, TILE), bf16),
            pltpu.VMEM((NY, 2, 2, PIECE, TILE), f32),
            pltpu.VMEM((NY, 2, 2, PIECE + CODES, TILE), i16),
            pltpu.VMEM((NY, 2, 2, PIECE + CODES, TILE), i16),
            pltpu.VMEM((NY, 2, PIECE + CODES, TILE), i16),
            pltpu.VMEM((NY, 2, PIECE + CODES, TILE), i16),
            pltpu.VMEM((NY, 2 * PIECE, TILE), f32),
            pltpu.VMEM((NY, NZ, CHUNK + CODES, TILE), i16),
            pltpu.VMEM((NY, NZ, CHUNK + CODES, TILE), i16),
            pltpu.VMEM((2, CHUNK, TILE), f32),
            pltpu.VMEM((2, CHUNK, TILE), f32),
            pltpu.VMEM((CHUNK, TILE), f32),
            pltpu.VMEM((CHUNK // 2, TILE), f32),
            pltpu.VMEM((CHUNK // 2, TILE), f32),
            dma((8,)),
            dma((8,)), dma((8,)),
            dma((4,)), dma((4,)),
            dma((8,)), dma((8,)),
            dma((8,)), dma((8,)),
            dma((NY * NZ,)), dma((NY * NZ,)),
            dma((2,)), dma((2,)),
            dma((1,)), dma((1,)),
        ],
        compiler_params=pltpu.CompilerParams(
            collective_id=0, has_side_effects=True, vmem_limit_bytes=56 * 2**20
        ),
    )(l_panels, u_panels, l_masks, u_masks, ancestor_tiles, initial)


def solution(mesh):
    return jax.shard_map(
        local,
        mesh=mesh,
        in_specs=(
            P("layer", None, "col"),
            P("layer", None, "col"),
            P("layer", None, None),
            P("layer", None, None),
            P(),
            P("layer", "col"),
        ),
        out_specs=P("layer", "col"),
        check_vma=False,
    )
```

time: 266 us -> 77.2 us (0.29); the launches traced: 261 us -> 77 us
  waiting for transfers between devices: 225 us -> 0 us
  Pallas kernels: 0 us -> 75.5 us
  between operations: 13.5 us -> 0.01 us
  matrix products: 10.6 us -> 0 us
  local copies, waits for them, and re-layouts: 8.05 us -> 1.47 us
  other arithmetic: 3.83 us -> 0 us
    reduce_scatter x1 -> x0, waiting for transfers between devices: 139 us -> none  [local(): summed = lax.psum_scatter(product, 'layer', scatter_dimension=0, tiled=True)]
    all_gather x1 -> x0, waiting for transfers between devices: 86.5 us -> none  [local(): full_panel = lax.all_gather(lpanel, 'col', axis=1, tiled=True)]
    pallas_call x0 -> x1, Pallas kernels: none -> 75.5 us  [local(): pl.pallas_call(kernel, out_shape=jax.ShapeDtypeStruct(initial.shape, f32)...]
    dot_general x2 -> x0, matrix products: 10.6 us -> none  [the longest x1 10.5 us: local(): product = jnp.dot(full_panel, upanel, preferred_element_type=jnp.float32)]
    broadcast_in_dim x5 -> x0, local copies, waits for them, and re-layouts: 5.19 us -> none  [the longest x4 5.08 us: expand_tiles(): return jnp.repeat(jnp.repeat(mask, TILE, 0), TILE, 1)]
  transfers between devices with their start and end apart: 2 -> 0, of which waited for: 2 -> 0; matrix products, arithmetic and copies ran while one was open for 1% -> 0% of each run, Pallas kernels for 0% -> 0%
where the time goes in v1:
time: 77.2 us; the launch traced here: 77 us
  Pallas kernels  75.5 us (98%)
  local copies, waits for them, and re-layouts  1.47 us (2%)
    pallas_call x1, Pallas kernels, local(): pl.pallas_call(kernel, out_shape=jax.ShapeDtypeStruct(initial.shape, f32)...  75.5 us

profile of v1, /device:TPU:1, one launch (start us, length us, event | category | flops | bytes accessed | tf_op | source)
XLA Modules:
  0.0 77.0 jit_solution(7227885317415385897)
XLA Ops:
  0.0 75.5 %shard_map.64 = f32[32,512]{1,0:T(8,128)} custom-call(bf16[1,2048,512]{2,1,0:T(8,128)(2,1)} %l_hbm.1, bf16[1,2048,512]{2,1,0:T(8,128)(2,1)} %u_hbm.1, s32[1,8,8]{2,1,0:T(8,128)} %lmask.1, s32[1,8,8]{2,1,0:T(8,128)} %umask.1, s32[8,8]{1,0:T(8,128)} %ancestor.1, f32[32,512]{1,0:T(8,128)} %initial.1), custom_call_target="tpu_custom_call" | custom-call | tf_op jit(solution)/shard_map/pallas_call | solution.py:271
  75.5 1.5 %copy.8 = f32[32,512]{1,0:T(8,128)} copy(f32[32,512]{1,0:T(8,128)} %shard_map.64) | data formatting | bytes 131072

commit v2 on v1

v2 whole, which is shorter than its diff:
```python
import jax
import jax.numpy as jnp
from jax import lax
from jax.experimental import pallas as pl
from jax.experimental.pallas import tpu as pltpu
from jax.sharding import PartitionSpec as P

MESH = pl.DeviceIdType.MESH
TILE = 256
NX, NY, NZ = 4, 4, 8
DEPTH = 512
PIECE = 256
CHUNK = 64
CODES = 16
COLS = 128
LEVELS = 32000.0
STEPS = 8.0


def encode(block, codes, where):
    rows, cols = block.shape
    top = jnp.maximum(jnp.max(jnp.abs(block), axis=0, keepdims=True), 2.0**-100)
    level = jnp.ceil(jnp.log2(top) * STEPS) + 1.0
    factor = jnp.exp2(level * (-1.0 / STEPS)) * LEVELS
    codes[(*where, pl.ds(0, rows), slice(None))] = jnp.round(block * factor).astype(jnp.int32).astype(jnp.int16)
    codes[(*where, pl.ds(rows, CODES), slice(None))] = (
        jnp.broadcast_to(level, (CODES, cols)).astype(jnp.int32).astype(jnp.int16)
    )


def decode(codes, where, rows):
    level = codes[(*where, pl.ds(rows, CODES), slice(None))].astype(jnp.int32).astype(jnp.float32)[0:1]
    factor = jnp.exp2(level * (1.0 / STEPS)) * (1.0 / LEVELS)
    return codes[(*where, pl.ds(0, rows), slice(None))].astype(jnp.int32).astype(jnp.float32) * factor


UNITS = ((0, 0), (0, 1), (1, 0), (1, 1), (3, 0), (3, 1), (2, 0), (2, 1))
TYPES = "ABAABBAA"
ORDER = (
    ("u", 0), ("u", 1), ("x1", 0), ("u", 2), ("u", 4), ("h", 1),
    ("x2", 0), ("x1", 2), ("u", 3), ("u", 5), ("x1", 1), ("h", 4),
    ("x2", 2), ("x1", 3), ("u", 6), ("x2", 1), ("z", 0), ("x1", 4),
    ("h", 5), ("x2", 3), ("x1", 6), ("u", 7), ("z", 2), ("x2", 4),
    ("x1", 5), ("z", 1), ("x2", 6), ("x1", 7), ("z", 3), ("z", 4),
    ("x2", 5), ("x2", 7), ("z", 6), ("z", 5), ("z", 7),
)
SPLIT = tuple(n for n, kind in enumerate(TYPES) if kind == "B")


def kernel(
    l_hbm, u_hbm, lmask, umask, ancestor, initial, out,
    lbuf, uown, ubuf, stage, hs, hr, part, x1s, x1r, x2s, x2r, ssum, zs, zr, ys, yr, total, cs, cr,
    in_sem, a_send, a_recv, l_send, l_recv, h_send, h_recv, x1_send, x1_recv, x2_send, x2_recv,
    z_send, z_recv, y_send, y_recv, c_send, c_recv,
):
    layer = lax.axis_index("layer")
    y = lax.axis_index("col")
    x = layer // (2 * NZ)
    z = (layer // 2) % NZ
    core = layer % 2
    xa = x + 1 - 2 * (x % 2)
    xb = 3 - x
    xd = 3 - xa
    odd = z % 2
    za = z + 1 - 2 * odd
    zb = (z + 2 * odd + NZ - 1) % NZ

    def at(x_, y_, z_, c_):
        return ((x_ * NZ + z_) * 2 + c_, y_)

    def ydev(step, k):
        return at(x, (y + step) % NY, z, (core + k) % 2)

    sibling = at(x, y, z, 1 - core)
    partners = [sibling]
    partners += [ydev(step, k) for step in (1, 2, 3) for k in (0, 1)]
    partners += [at(xa, y, z, core), at(xb, y, z, core)]
    partners += [at(x, y, (z + i) % NZ, core) for i in range(1, NZ)]
    partners += [at(x, (y + 2) % NY, (z + i) % NZ, core) for i in range(1, NZ)]

    def rows_of(first, count):
        return pl.ds(pl.multiple_of(first, count), count)

    u_order = [(y + step) % NY for step in (1, 3, 2, 0)]
    l_order = [xd, xa, xb, x]
    u_in = [
        pltpu.make_async_copy(u_hbm.at[0, rows_of(b * DEPTH, DEPTH)], uown.at[rows_of(b * DEPTH, DEPTH)], in_sem.at[n])
        for n, b in enumerate(u_order)
    ]
    l_in = [
        pltpu.make_async_copy(l_hbm.at[0, rows_of(b * DEPTH, DEPTH)], lbuf.at[0, rows_of(b * DEPTH, DEPTH)], in_sem.at[4 + n])
        for n, b in enumerate(l_order)
    ]
    for n in (0, 1, 3):
        u_in[n].start()
    for n in range(4):
        l_in[n].start()
    u_in[2].start()
    barrier = pltpu.get_barrier_semaphore()
    for partner in partners:
        pl.semaphore_signal(barrier, inc=1, device_id=partner, device_id_type=MESH)

    def mask_tiles(ref, where, mask, block):
        for t in range(2):
            rows = rows_of(block * DEPTH + t * TILE, TILE)
            for h in range(2):
                keep = mask[0, block * 2 + t, y * 2 + h].astype(jnp.float32)
                spot = (*where, rows, pl.ds(h * TILE, TILE))
                ref[spot] = ref[spot] * jnp.full((TILE, TILE), keep).astype(jnp.bfloat16)

    def number(s, h):
        return UNITS.index((s, h))

    def send_u(step, k, h):
        n = number((NY - step) % NY, h)
        cols = pl.ds(pl.multiple_of((core + k) % 2 * TILE + h * COLS, COLS), COLS)
        return pltpu.make_async_remote_copy(
            uown.at[rows_of((y + step) % NY * DEPTH, DEPTH), cols], ubuf.at[n, k],
            a_send.at[n * 2 + k], a_recv.at[n * 2 + k], device_id=ydev(step, k), device_id_type=MESH,
        )

    def send_l(n):
        rows = rows_of(l_order[n] * DEPTH, DEPTH)
        return pltpu.make_async_remote_copy(
            lbuf.at[0, rows], lbuf.at[1, rows], l_send.at[n], l_recv.at[n], device_id=sibling, device_id_type=MESH,
        )

    for n in range(2):
        u_in[n].wait()
        mask_tiles(uown, (), umask, u_order[n])
    pl.semaphore_wait(barrier, len(partners))
    for h in range(2):
        for step in (1, 3):
            for k in range(2):
                send_u(step, k, h).start()
    u_in[3].wait()
    mask_tiles(uown, (), umask, y)
    for h in range(2):
        send_u(0, 1, h).start()
    for n in range(4):
        l_in[n].wait()
        mask_tiles(lbuf, (0,), lmask, l_order[n])
        send_l(n).start()
    u_in[2].wait()
    mask_tiles(uown, (), umask, u_order[2])
    for h in range(2):
        for k in range(2):
            send_u(2, k, h).start()
        cols = pl.ds(pl.multiple_of(core * TILE + h * COLS, COLS), COLS)
        ubuf[number(0, h), 0] = uown[rows_of(y * DEPTH, DEPTH), cols]

    def product(n, goal, q):
        rows = rows_of(goal * 2 * PIECE + q * PIECE, PIECE)
        return jnp.dot(lbuf[0, rows], ubuf[n, 0], preferred_element_type=jnp.float32) + jnp.dot(
            lbuf[1, rows], ubuf[n, 1], preferred_element_type=jnp.float32
        )

    def rows_in(n):
        return PIECE // 2 if TYPES[n] == "B" else PIECE

    def h_copy(n, q, j):
        b = SPLIT.index(n)
        sem = (b * 2 + q) * 4 + j
        return pltpu.make_async_remote_copy(
            hs.at[b, q, j], hr.at[b, q, j], h_send.at[sem], h_recv.at[sem],
            device_id=at(x, y, zb if q else za, core), device_id_type=MESH,
        )

    def x1_copy(n, q, i):
        sem = (n * 2 + q) * 2 + i
        rows = pl.ds(0, rows_in(n) + CODES)
        return pltpu.make_async_remote_copy(
            x1s.at[n, q, i, rows], x1r.at[n, q, i, rows], x1_send.at[sem], x1_recv.at[sem],
            device_id=at(xb if q else xa, y, z, core), device_id_type=MESH,
        )

    def x2_copy(n, q):
        sem = n * 2 + q
        rows = pl.ds(0, rows_in(n) + CODES)
        return pltpu.make_async_remote_copy(
            x2s.at[n, q, rows], x2r.at[n, q, rows], x2_send.at[sem], x2_recv.at[sem],
            device_id=at(xa if q else xb, y, z, core), device_id_type=MESH,
        )

    def z_copy(n, i):
        sem = n * NZ + i
        return pltpu.make_async_remote_copy(
            zs.at[n, i], zr.at[n, i], z_send.at[sem], z_recv.at[sem],
            device_id=at(x, (y + 2) % NY if UNITS[n][0] == 2 else y, (z + i) % NZ, core), device_id_type=MESH,
        )

    def y_copy(n):
        return pltpu.make_async_remote_copy(
            ys.at[n - 2], yr.at[n - 2], y_send.at[n - 2], y_recv.at[n - 2], device_id=ydev(UNITS[n][0], 0), device_id_type=MESH,
        )

    def z_steps(n):
        steps = (4, 2, 6) if TYPES[n] == "B" else (4, 3, 5, 2, 6, 1, 7)
        return steps + ((0,) if UNITS[n][0] == 2 else ())

    def arrive(n):
        s, h = UNITS[n]
        for k in (1,) if s == 0 else (0, 1):
            send_u((NY - s) % NY, k, h).wait_recv()
        if n == 0:
            for m in range(4):
                send_l(m).wait_recv()

    def multiply(n):
        arrive(n)
        if TYPES[n] == "A":
            for i in (1, 0):
                for q in range(2):
                    goal = xd if i else (xb if q else xa)
                    encode(product(n, goal, q), x1s, (n, q, i))
                    x1_copy(n, q, i).start()
            for i in (1, 0):
                for q in range(2):
                    part[n, q, i] = product(n, (xa if q else xb) if i else x, q)
        else:
            b = SPLIT.index(n)
            for j, goal in enumerate(l_order):
                for q in range(2):
                    stage[b, q, j] = product(n, goal, q)
                    encode(parity(b, q, j, 1 - odd), hs, (b, q, j))
                    h_copy(n, q, j).start()

    def parity(b, q, j, which):
        chunks = [stage[b, q, j, rows_of((which + 2 * t) * CHUNK, CHUNK)] for t in range(2)]
        return jnp.concatenate(chunks, axis=0)

    def after_h(n):
        b = SPLIT.index(n)
        half = PIECE // 2

        def summed(q, j):
            h_copy(n, q, j).wait_recv()
            return parity(b, q, j, odd) + decode(hr, (b, q, j), half)

        for q in range(2):
            encode(summed(q, 0), x1s, (n, q, 1))
            x1_copy(n, q, 1).start()
        for q in range(2):
            encode(summed(q, 2 if q else 1), x1s, (n, q, 0))
            x1_copy(n, q, 0).start()
        for q in range(2):
            part[n, q, 1, pl.ds(0, half)] = summed(q, 1 if q else 2)
            part[n, q, 0, pl.ds(0, half)] = summed(q, 3)

    def after_x1(n):
        rows = rows_in(n)
        for q in range(2):
            x1_copy(n, q, 1).wait_recv()
            encode(part[n, q, 1, pl.ds(0, rows)] + decode(x1r, (n, q, 1), rows), x2s, (n, q))
            x2_copy(n, q).start()

    def after_x2(n):
        rows = rows_in(n)
        for q in range(2):
            x1_copy(n, q, 0).wait_recv()
            x2_copy(n, q).wait_recv()
            ssum[n, pl.ds(q * rows, rows)] = (
                part[n, q, 0, pl.ds(0, rows)] + decode(x1r, (n, q, 0), rows) + decode(x2r, (n, q), rows)
            )
        for i in z_steps(n):
            encode(own_rows(n, (z + i) % NZ), zs, (n, i))
            z_copy(n, i).start()

    def own_rows(n, goal):
        spot = goal // 2 if TYPES[n] == "B" else goal
        return ssum[n, rows_of(spot * CHUNK, CHUNK)]

    def after_z(n):
        s, h = UNITS[n]
        result = None if s == 2 else own_rows(n, z)
        for i in reversed(z_steps(n)):
            z_copy(n, i).wait_recv()
            piece = decode(zr, (n, i), CHUNK)
            result = piece if result is None else result + piece
        if s in (1, 3):
            ys[n - 2] = result
            y_copy(n).start()
        else:
            total[s // 2, :, pl.ds(h * COLS, COLS)] = result

    actions = {"u": multiply, "h": after_h, "x1": after_x1, "x2": after_x2, "z": after_z}
    for action, n in ORDER:
        actions[action](n)

    for n in range(2, 6):
        y_copy(n).wait_recv()
    for h in range(2):
        cols = pl.ds(h * COLS, COLS)
        total[0, :, cols] = total[0, :, cols] + total[1, :, cols] + yr[h] + yr[2 + h]
    half = CHUNK // 2
    cs[...] = total[0, rows_of((1 - core) * half, half)]
    across = pltpu.make_async_remote_copy(cs, cr, c_send.at[0], c_recv.at[0], device_id=sibling, device_id_type=MESH)
    across.start()

    def finish(side, value):
        keep = ancestor[layer // (TILE // half), y * 2 + side].astype(jnp.float32)
        cols = pl.ds(pl.multiple_of(side * TILE, TILE), TILE)
        out[:, cols] = initial[:, cols] - keep * value

    finish(core, total[0, rows_of(core * half, half)])

    for h in range(2):
        for step in (1, 3, 2):
            for k in range(2):
                send_u(step, k, h).wait_send()
        send_u(0, 1, h).wait_send()
    for n in range(4):
        send_l(n).wait_send()
    for n in range(len(UNITS)):
        for q in range(2):
            if TYPES[n] == "B":
                for j in range(4):
                    h_copy(n, q, j).wait_send()
            x1_copy(n, q, 0).wait_send()
            x1_copy(n, q, 1).wait_send()
            x2_copy(n, q).wait_send()
        for i in z_steps(n):
            z_copy(n, i).wait_send()
        if 2 <= n < 6:
            y_copy(n).wait_send()
    across.wait_recv()
    finish(1 - core, cr[...])
    across.wait_send()


def local(l_panels, u_panels, l_masks, u_masks, ancestor_tiles, initial):
    any_spec = pl.BlockSpec(memory_space=pl.ANY)
    smem = pl.BlockSpec(memory_space=pltpu.SMEM)
    vmem = pl.BlockSpec(memory_space=pltpu.VMEM)
    dma = pltpu.SemaphoreType.DMA
    bf16, f32, i16 = jnp.bfloat16, jnp.float32, jnp.int16
    units, splits = len(UNITS), max(len(SPLIT), 1)
    halves = PIECE // 2 + CODES
    pairs = [8 * splits, 4 * units, 2 * units, NZ * units, 4, 1]
    return pl.pallas_call(
        kernel,
        out_shape=jax.ShapeDtypeStruct(initial.shape, f32),
        in_specs=[any_spec, any_spec, smem, smem, smem, vmem],
        out_specs=vmem,
        scratch_shapes=[
            pltpu.VMEM((2, 2048, DEPTH), bf16),
            pltpu.VMEM((2048, DEPTH), bf16),
            pltpu.VMEM((units, 2, DEPTH, COLS), bf16),
            pltpu.VMEM((splits, 2, 4, PIECE, COLS), f32),
            pltpu.VMEM((splits, 2, 4, halves, COLS), i16),
            pltpu.VMEM((splits, 2, 4, halves, COLS), i16),
            pltpu.VMEM((units, 2, 2, PIECE, COLS), f32),
            pltpu.VMEM((units, 2, 2, PIECE + CODES, COLS), i16),
            pltpu.VMEM((units, 2, 2, PIECE + CODES, COLS), i16),
            pltpu.VMEM((units, 2, PIECE + CODES, COLS), i16),
            pltpu.VMEM((units, 2, PIECE + CODES, COLS), i16),
            pltpu.VMEM((units, 2 * PIECE, COLS), f32),
            pltpu.VMEM((units, NZ, CHUNK + CODES, COLS), i16),
            pltpu.VMEM((units, NZ, CHUNK + CODES, COLS), i16),
            pltpu.VMEM((4, CHUNK, COLS), f32),
            pltpu.VMEM((4, CHUNK, COLS), f32),
            pltpu.VMEM((2, CHUNK, TILE), f32),
            pltpu.VMEM((CHUNK // 2, TILE), f32),
            pltpu.VMEM((CHUNK // 2, TILE), f32),
            dma((8,)),
            dma((2 * units,)), dma((2 * units,)),
            dma((4,)), dma((4,)),
            *[dma((count,)) for count in pairs for _ in range(2)],
        ],
        compiler_params=pltpu.CompilerParams(
            collective_id=0, has_side_effects=True, vmem_limit_bytes=56 * 2**20
        ),
    )(l_panels, u_panels, l_masks, u_masks, ancestor_tiles, initial)


def solution(mesh):
    return jax.shard_map(
        local,
        mesh=mesh,
        in_specs=(
            P("layer", None, "col"),
            P("layer", None, "col"),
            P("layer", None, None),
            P("layer", None, None),
            P(),
            P("layer", "col"),
        ),
        out_specs=P("layer", "col"),
        check_vma=False,
    )
```

time: 77.2 us -> 65.2 us (0.84)
  Pallas kernels: 75.5 us -> 63.6 us
    pallas_call x1, Pallas kernels: 75.5 us -> 63.6 us  [local(): pl.pallas_call(kernel, out_shape=jax.ShapeDtypeStruct(initial.shape, f32)...]
where the time goes in v2:
time: 65.2 us; the launch traced here: 65.1 us
  Pallas kernels  63.6 us (98%)
  local copies, waits for them, and re-layouts  1.47 us (2%)
    pallas_call x1, Pallas kernels, local(): pl.pallas_call(kernel, out_shape=jax.ShapeDtypeStruct(initial.shape, f32)...  63.6 us
    unnamed x1, local copies, waits for them, and re-layouts  1.47 us

profile of v2, /device:TPU:1, one launch (start us, length us, event | category | flops | bytes accessed | tf_op | source)
XLA Modules:
  0.0 65.1 jit_solution(9433008582046371434)
XLA Ops:
  0.0 63.6 %shard_map.64 = f32[32,512]{1,0:T(8,128)} custom-call(bf16[1,2048,512]{2,1,0:T(8,128)(2,1)} %l_hbm.1, bf16[1,2048,512]{2,1,0:T(8,128)(2,1)} %u_hbm.1, s32[1,8,8]{2,1,0:T(8,128)} %lmask.1, s32[1,8,8]{2,1,0:T(8,128)} %umask.1, s32[8,8]{1,0:T(8,128)} %ancestor.1, f32[32,512]{1,0:T(8,128)} %initial.1), custom_call_target="tpu_custom_call" | custom-call | tf_op jit(solution)/shard_map/pallas_call | solution.py:340
  63.6 1.5 %copy.8 = f32[32,512]{1,0:T(8,128)} copy(f32[32,512]{1,0:T(8,128)} %shard_map.64) | data formatting | bytes 131072

commit v3 on v2

--- a/solution.py
+++ b/solution.py
@@ -35,20 +35,21 @@
 
 
 UNITS = ((0, 0), (0, 1), (1, 0), (1, 1), (3, 0), (3, 1), (2, 0), (2, 1))
-TYPES = "ABAABBAA"
+TYPES = "ABABBABA"
 ORDER = (
     ("u", 0), ("u", 1), ("x1", 0), ("u", 2), ("u", 4), ("h", 1),
     ("x2", 0), ("x1", 2), ("u", 3), ("u", 5), ("x1", 1), ("h", 4),
-    ("x2", 2), ("x1", 3), ("u", 6), ("x2", 1), ("z", 0), ("x1", 4),
-    ("h", 5), ("x2", 3), ("x1", 6), ("u", 7), ("z", 2), ("x2", 4),
-    ("x1", 5), ("z", 1), ("x2", 6), ("x1", 7), ("z", 3), ("z", 4),
-    ("x2", 5), ("x2", 7), ("z", 6), ("z", 5), ("z", 7),
+    ("x2", 2), ("x1", 5), ("u", 6), ("z", 0), ("x2", 1), ("h", 3),
+    ("x1", 4), ("x2", 5), ("u", 7), ("x1", 3), ("z", 2), ("x2", 4),
+    ("h", 6), ("x1", 7), ("x2", 3), ("z", 1), ("x1", 6), ("x2", 7),
+    ("z", 5), ("x2", 6), ("z", 4), ("z", 3), ("z", 7), ("z", 6),
 )
 SPLIT = tuple(n for n, kind in enumerate(TYPES) if kind == "B")
 
 
 def kernel(
-    l_hbm, u_hbm, lmask, umask, ancestor, initial, out,
+    l_hbm, u_hbm, lmask_hbm, umask_hbm, ancestor_hbm, initial_hbm, out,
+    lmask, umask, ancestor, initial,
     lbuf, uown, ubuf, stage, hs, hr, part, x1s, x1r, x2s, x2r, ssum, zs, zr, ys, yr, total, cs, cr,
     in_sem, a_send, a_recv, l_send, l_recv, h_send, h_recv, x1_send, x1_recv, x2_send, x2_recv,
     z_send, z_recv, y_send, y_recv, c_send, c_recv,
@@ -81,6 +82,10 @@
     def rows_of(first, count):
         return pl.ds(pl.multiple_of(first, count), count)
 
+    barrier = pltpu.get_barrier_semaphore()
+    for partner in partners:
+        pl.semaphore_signal(barrier, inc=1, device_id=partner, device_id_type=MESH)
+
     u_order = [(y + step) % NY for step in (1, 3, 2, 0)]
     l_order = [xd, xa, xb, x]
     u_in = [
@@ -91,14 +96,21 @@
         pltpu.make_async_copy(l_hbm.at[0, rows_of(b * DEPTH, DEPTH)], lbuf.at[0, rows_of(b * DEPTH, DEPTH)], in_sem.at[4 + n])
         for n, b in enumerate(l_order)
     ]
+    small = [
+        pltpu.make_async_copy(source, target, in_sem.at[8 + n])
+        for n, (source, target) in enumerate(
+            ((umask_hbm, umask), (lmask_hbm, lmask), (ancestor_hbm, ancestor), (initial_hbm, initial))
+        )
+    ]
+    small[0].start()
+    small[1].start()
     for n in (0, 1, 3):
         u_in[n].start()
     for n in range(4):
         l_in[n].start()
     u_in[2].start()
-    barrier = pltpu.get_barrier_semaphore()
-    for partner in partners:
-        pl.semaphore_signal(barrier, inc=1, device_id=partner, device_id_type=MESH)
+    small[2].start()
+    small[3].start()
 
     def mask_tiles(ref, where, mask, block):
         for t in range(2):
@@ -125,29 +137,31 @@
             lbuf.at[0, rows], lbuf.at[1, rows], l_send.at[n], l_recv.at[n], device_id=sibling, device_id_type=MESH,
         )
 
-    for n in range(2):
+    small[0].wait()
+    for n in (0, 1, 3):
         u_in[n].wait()
         mask_tiles(uown, (), umask, u_order[n])
+    small[1].wait()
+    for n in range(4):
+        l_in[n].wait()
+        mask_tiles(lbuf, (0,), lmask, l_order[n])
     pl.semaphore_wait(barrier, len(partners))
     for h in range(2):
         for step in (1, 3):
             for k in range(2):
                 send_u(step, k, h).start()
-    u_in[3].wait()
-    mask_tiles(uown, (), umask, y)
+        send_u(0, 1, h).start()
+        send_l(h).start()
+    for n in (2, 3):
+        send_l(n).start()
     for h in range(2):
-        send_u(0, 1, h).start()
-    for n in range(4):
-        l_in[n].wait()
-        mask_tiles(lbuf, (0,), lmask, l_order[n])
-        send_l(n).start()
+        cols = pl.ds(pl.multiple_of(core * TILE + h * COLS, COLS), COLS)
+        ubuf[number(0, h), 0] = uown[rows_of(y * DEPTH, DEPTH), cols]
     u_in[2].wait()
     mask_tiles(uown, (), umask, u_order[2])
     for h in range(2):
         for k in range(2):
             send_u(2, k, h).start()
-        cols = pl.ds(pl.multiple_of(core * TILE + h * COLS, COLS), COLS)
-        ubuf[number(0, h), 0] = uown[rows_of(y * DEPTH, DEPTH), cols]
 
     def product(n, goal, q):
         rows = rows_of(goal * 2 * PIECE + q * PIECE, PIECE)
@@ -202,9 +216,10 @@
         s, h = UNITS[n]
         for k in (1,) if s == 0 else (0, 1):
             send_u((NY - s) % NY, k, h).wait_recv()
-        if n == 0:
-            for m in range(4):
-                send_l(m).wait_recv()
+
+    def l_ready(n, m):
+        if n == ORDER[0][1] and m is not None:
+            send_l(m).wait_recv()
 
     def multiply(n):
         arrive(n)
@@ -212,14 +227,17 @@
             for i in (1, 0):
                 for q in range(2):
                     goal = xd if i else (xb if q else xa)
+                    l_ready(n, (0, None, 1, 2)[2 * (1 - i) + q])
                     encode(product(n, goal, q), x1s, (n, q, i))
                     x1_copy(n, q, i).start()
+            l_ready(n, 3)
             for i in (1, 0):
                 for q in range(2):
                     part[n, q, i] = product(n, (xa if q else xb) if i else x, q)
         else:
             b = SPLIT.index(n)
             for j, goal in enumerate(l_order):
+                l_ready(n, j)
                 for q in range(2):
                     stage[b, q, j] = product(n, goal, q)
                     encode(parity(b, q, j, 1 - odd), hs, (b, q, j))
@@ -296,6 +314,9 @@
     cs[...] = total[0, rows_of((1 - core) * half, half)]
     across = pltpu.make_async_remote_copy(cs, cr, c_send.at[0], c_recv.at[0], device_id=sibling, device_id_type=MESH)
     across.start()
+
+    small[2].wait()
+    small[3].wait()
 
     def finish(side, value):
         keep = ancestor[layer // (TILE // half), y * 2 + side].astype(jnp.float32)
@@ -330,7 +351,6 @@
 
 def local(l_panels, u_panels, l_masks, u_masks, ancestor_tiles, initial):
     any_spec = pl.BlockSpec(memory_space=pl.ANY)
-    smem = pl.BlockSpec(memory_space=pltpu.SMEM)
     vmem = pl.BlockSpec(memory_space=pltpu.VMEM)
     dma = pltpu.SemaphoreType.DMA
     bf16, f32, i16 = jnp.bfloat16, jnp.float32, jnp.int16
@@ -340,9 +360,13 @@
     return pl.pallas_call(
         kernel,
         out_shape=jax.ShapeDtypeStruct(initial.shape, f32),
-        in_specs=[any_spec, any_spec, smem, smem, smem, vmem],
+        in_specs=[any_spec] * 6,
         out_specs=vmem,
         scratch_shapes=[
+            pltpu.SMEM(l_masks.shape, jnp.int32),
+            pltpu.SMEM(u_masks.shape, jnp.int32),
+            pltpu.SMEM(ancestor_tiles.shape, jnp.int32),
+            pltpu.VMEM(initial.shape, f32),
             pltpu.VMEM((2, 2048, DEPTH), bf16),
             pltpu.VMEM((2048, DEPTH), bf16),
             pltpu.VMEM((units, 2, DEPTH, COLS), bf16),
@@ -362,7 +386,7 @@
             pltpu.VMEM((2, CHUNK, TILE), f32),
             pltpu.VMEM((CHUNK // 2, TILE), f32),
             pltpu.VMEM((CHUNK // 2, TILE), f32),
-            dma((8,)),
+            dma((12,)),
             dma((2 * units,)), dma((2 * units,)),
             dma((4,)), dma((4,)),
             *[dma((count,)) for count in pairs for _ in range(2)],

time: 65.2 us -> 63.5 us (0.974)
  Pallas kernels: 63.6 us -> 61.9 us
    pallas_call x1, Pallas kernels: 63.6 us -> 61.9 us  [local(): pl.pallas_call(kernel, out_shape=jax.ShapeDtypeStruct(initial.shape, f32)...]
where the time goes in v3:
time: 63.5 us; the launch traced here: 63.4 us
  Pallas kernels  61.9 us (97%)
  local copies, waits for them, and re-layouts  1.47 us (2%)
    pallas_call x1, Pallas kernels, local(): pl.pallas_call(kernel, out_shape=jax.ShapeDtypeStruct(initial.shape, f32)...  61.9 us
    unnamed x1, local copies, waits for them, and re-layouts  1.47 us

profile of v3, /device:TPU:1, one launch (start us, length us, event | category | flops | bytes accessed | tf_op | source)
XLA Modules:
  0.0 63.4 jit_solution(12565549897157164319)
XLA Ops:
  0.0 61.9 %shard_map.64 = f32[32,512]{1,0:T(8,128)} custom-call(bf16[1,2048,512]{2,1,0:T(8,128)(2,1)} %l_hbm.1, bf16[1,2048,512]{2,1,0:T(8,128)(2,1)} %u_hbm.1, s32[1,8,8]{2,1,0:T(8,128)} %lmask_hbm.1, s32[1,8,8]{2,1,0:T(8,128)} %umask_hbm.1, s32[8,8]{1,0:T(8,128)} %ancestor_hbm.1, f32[32,512]{1,0:T(8,128)} %initial_hbm.1), custom_call_target="tpu_custom_call" | custom-call | tf_op jit(solution)/shard_map/pallas_call | solution.py:360
  61.9 1.5 %copy.8 = f32[32,512]{1,0:T(8,128)} copy(f32[32,512]{1,0:T(8,128)} %shard_map.64) | data formatting | bytes 131072
